TPU v7x, 32 devices: a whole 2x2x4 slice. The times are simulated.
32 devices in a mesh: blk: 8 (over z, x), col: 4 (over y, core).
Axes of the slice: x: 2, y: 2, z: 4, core: 2. Of those that a mesh axis runs over, the one named last changes fastest.
Arguments:
- density: float32 [2048, 1024], P('blk'), may hold values from -0.1875 to 0.1875
- occupied_p: int32 [16, 8], P('blk'), may hold values 0 or 1
- hamil_dens: float32 [1024, 2048], P('blk', 'col'), may hold values from -6 to 6
- occupied_hp: int32 [8, 16], P('blk', 'col'), may hold values 0 or 1
- window_sizes: int32 [8], replicated, may hold values from 64 to 128
- row_window_sizes: int32 [16], replicated, may hold values from 64 to 128
- slab_index: int32 [16], P('col'), may hold values from 0 to 781
- group_sizes: int32 [782], replicated, may hold values from 64 to 128
Outputs:
- product: float32 [2048, 2048], P('blk', 'col')
- norm_sq: float32 [], replicated
All inputs are finite; a program needn't handle non-finite values. No bound on the sum of `occupied_p` or of `occupied_hp` on one device may be relied on, other than what follows from the above.
Results may differ from a plain program's by a relative error of at most 0.000068.
Values sent between devices are 32-bit elements; how exact they have to be, the bound alone decides.
A program may use at most 64 MiB of HBM per device.

v0:
```python
import jax
import jax.numpy as jnp
from jax import lax
from jax.sharding import PartitionSpec as P


def shifted(value, axis, steps):
    count = lax.axis_size(axis)
    pairs = [(source, (source + steps) % count) for source in range(count)]
    return lax.ppermute(value, axis, pairs)


def per_device(
    density,
    occupied_p,
    hamil_dens,
    occupied_hp,
    window_sizes,
    row_window_sizes,
    slab_index,
    group_sizes,
):
    block = hamil_dens.shape[0]
    row_blocks = occupied_p.shape[0]
    inner_blocks = occupied_p.shape[1]
    count = lax.axis_size("blk")
    mine = lax.axis_index("blk")
    offsets = jnp.arange(block, dtype=jnp.int32)
    inner_live = (offsets[None, :] < window_sizes[:, None]).astype(jnp.float32)
    own_inner = lax.dynamic_index_in_dim(inner_live, mine, 0, keepdims=False)
    own_sizes = lax.dynamic_slice_in_dim(row_window_sizes, mine * row_blocks, row_blocks, 0)
    row_live = (offsets[None, :] < own_sizes[:, None]).astype(jnp.float32)
    groups = jnp.arange(group_sizes.shape[0], dtype=jnp.int32)
    slab_sizes = jnp.sum(
        jnp.where(slab_index[:, None] == groups[None, :], group_sizes[None, :], 0), axis=1
    )
    col_live = (offsets[None, :] < slab_sizes[:, None]).astype(jnp.float32)
    occ_p = occupied_p.astype(jnp.float32)
    p_mask = occ_p[:, None, :, None] * row_live[:, :, None, None] * inner_live[None, None, :, :]
    p_eff = (density.reshape(row_blocks, block, inner_blocks, block) * p_mask).reshape(
        row_blocks * block, inner_blocks * block
    )
    occ_hp = occupied_hp[0].astype(jnp.float32)
    hp_cols = (occ_hp[:, None] * col_live).reshape(-1)
    hp_eff = hamil_dens * hp_cols[None, :] * own_inner[:, None]

    def panel_of(source):
        return lax.dynamic_slice_in_dim(p_eff, source * block, block, 1)

    def times(left, right):
        return jnp.dot(
            left, right, precision=lax.Precision.HIGHEST, preferred_element_type=jnp.float32
        )

    first = times(panel_of(mine), hp_eff)

    def step_one(step, carry):
        total, current = carry
        current = shifted(current, "blk", 1)
        source = (mine - step) % count
        return (total + times(panel_of(source), current), current)

    product, unused = lax.fori_loop(1, count, step_one, (first, hp_eff))
    norm_sq = lax.psum(jnp.sum(product * product), ("blk", "col"))
    return (product, norm_sq)


def solution(mesh):
    return jax.shard_map(
        per_device,
        mesh=mesh,
        in_specs=(
            P("blk", None),
            P("blk", None),
            P("blk", "col"),
            P("blk", "col"),
            P(),
            P(),
            P("col"),
            P(),
        ),
        out_specs=(P("blk", "col"), P()),
        check_vma=False,
    )
```

profile of v0, /device:TPU:0, one launch (start us, length us, event | category | flops | bytes accessed | tf_op | source)
XLA Modules:
  0.0 118.7 jit_solution(6489901492230703361)
XLA Ops:
  0.6 0.8 dynamic_slice.20
  1.5 0.7 convert_bitcast_fusion
  2.1 0.1 compare_convert_fusion
  2.2 0.9 select_reduce_fusion
  3.1 0.1 select_bitcast_fusion
  3.1 0.7 convert_element_type.30
  3.8 0.7 fusion.5
  4.6 0.7 lt.105
  5.3 0.1 broadcast_multiply_fusion
  5.4 1.0 multiply_multiply_fusion
  6.4 0.3 mul.89
  6.8 0.3 fusion.2
  7.1 0.6 fusion.3
  7.7 73.2 %while.17 = (s32[]{:T(128)}, f32[256,512]{1,0:T(8,128)S(1)}, f32[128,512]{1,0:T(8,128)S(1)}, s32[]{:T(128)}, f32[256,1024]{1,0:T(8,128)S(1)}, /*index=5*/s32[]{:...) while((s32[]{:T(128)}, f32[256,512]{1,0:T(8,128)S(1)}, f32[128,512]{1,0:T(8,128)S(1)}, ...), condition=%wide.region_2.3_spmd, body=%wide.region_1.2_spmd.sunk | while | flops 201457680 | bytes 3014976 | solution.py:63
  7.7 3.0 %collective-permute-start = (f32[128,512]{1,0:T(8,128)S(1)}, f32[128,512]{1,0:T(8,128)S(1)}, u32[]{:S(2)}, u32[]{:S(2)}) collective-permute-start(f32[128,512]{1,0:T(8,128)S(1)} %get-tuple-element.190), channel_id=1, source_target_pairs={{0,4},{4,8},{8,12},{12,16},{16,20},{20,24},{24,28},{28,0},{1,5},{5... | collective-permute-start | bytes 786440 | tf_op jit(solution)/shard_map/while/body/eval_jaxpr/ppermute | solution.py:10
  10.7 9.3 %collective-permute-done = f32[128,512]{1,0:T(8,128)S(1)} collective-permute-done((f32[128,512]{1,0:T(8,128)S(1)}, f32[128,512]{1,0:T(8,128)S(1)}, u32[]{:S(2)}, u32[]{:S(2)}) %collective-permute-start) | collective-permute-done | bytes 262176 | tf_op jit(solution)/shard_map/while/body/eval_jaxpr/ppermute | solution.py:10
  20.1 0.6 convolution_add_fusion.2
  20.7 0.1 collective-permute-start
  20.8 10.2 %collective-permute-done = f32[128,512]{1,0:T(8,128)S(1)} collective-permute-done((f32[128,512]{1,0:T(8,128)S(1)}, f32[128,512]{1,0:T(8,128)S(1)}, u32[]{:S(2)}, u32[]{:S(2)}) %collective-permute-start) | collective-permute-done | bytes 262176 | tf_op jit(solution)/shard_map/while/body/eval_jaxpr/ppermute | solution.py:10
  31.0 0.6 convolution_add_fusion.2
  31.7 9.2 %collective-permute-done = f32[128,512]{1,0:T(8,128)S(1)} collective-permute-done((f32[128,512]{1,0:T(8,128)S(1)}, f32[128,512]{1,0:T(8,128)S(1)}, u32[]{:S(2)}, u32[]{:S(2)}) %collective-permute-start) | collective-permute-done | bytes 262176 | tf_op jit(solution)/shard_map/while/body/eval_jaxpr/ppermute | solution.py:10
  41.0 0.6 convolution_add_fusion.2
  41.7 9.0 %collective-permute-done = f32[128,512]{1,0:T(8,128)S(1)} collective-permute-done((f32[128,512]{1,0:T(8,128)S(1)}, f32[128,512]{1,0:T(8,128)S(1)}, u32[]{:S(2)}, u32[]{:S(2)}) %collective-permute-start) | collective-permute-done | bytes 262176 | tf_op jit(solution)/shard_map/while/body/eval_jaxpr/ppermute | solution.py:10
  50.8 0.6 convolution_add_fusion.2
  51.6 9.0 %collective-permute-done = f32[128,512]{1,0:T(8,128)S(1)} collective-permute-done((f32[128,512]{1,0:T(8,128)S(1)}, f32[128,512]{1,0:T(8,128)S(1)}, u32[]{:S(2)}, u32[]{:S(2)}) %collective-permute-start) | collective-permute-done | bytes 262176 | tf_op jit(solution)/shard_map/while/body/eval_jaxpr/ppermute | solution.py:10
  60.6 0.7 convolution_add_fusion.2
  61.4 9.0 %collective-permute-done = f32[128,512]{1,0:T(8,128)S(1)} collective-permute-done((f32[128,512]{1,0:T(8,128)S(1)}, f32[128,512]{1,0:T(8,128)S(1)}, u32[]{:S(2)}, u32[]{:S(2)}) %collective-permute-start) | collective-permute-done | bytes 262176 | tf_op jit(solution)/shard_map/while/body/eval_jaxpr/ppermute | solution.py:10
  70.4 0.6 convolution_add_fusion.2
  71.2 9.0 %collective-permute-done = f32[128,512]{1,0:T(8,128)S(1)} collective-permute-done((f32[128,512]{1,0:T(8,128)S(1)}, f32[128,512]{1,0:T(8,128)S(1)}, u32[]{:S(2)}, u32[]{:S(2)}) %collective-permute-start) | collective-permute-done | bytes 262176 | tf_op jit(solution)/shard_map/while/body/eval_jaxpr/ppermute | solution.py:10
  80.2 0.6 convolution_add_fusion.2
  80.9 0.7 multiply_reduce_fusion
  81.6 37.1 %psum.7 = f32[]{:T(128)} all-reduce(f32[]{:T(128)} %multiply_reduce_fusion), channel_id=1, replica_groups=mesh['blk'=8,'col'=4] {'blk','col'}, use_global_device_ids=true, to_apply=%region_4.5 | all-reduce | flops 1 | bytes 8 | tf_op jit(solution)/shard_map/psum | solution.py:64
  (18 shorter events, 0.4 us)
Async XLA Ops:
  0.6 6.1 %copy-start.1 = (f32[256,1024]{1,0:T(8,128)S(1)}, f32[256,1024]{1,0:T(8,128)}, u32[]{:S(2)}) copy-start(f32[256,1024]{1,0:T(8,128)} %param.10) | copy-start | bytes 3145732
  7.7 12.3 %collective-permute-start = (f32[128,512]{1,0:T(8,128)S(1)}, f32[128,512]{1,0:T(8,128)S(1)}, u32[]{:S(2)}, u32[]{:S(2)}) collective-permute-start(f32[128,512]{1,0:T(8,128)S(1)} %get-tuple-element.190), channel_id=1, source_target_pairs={{0,4},{4,8},{8,12},{12,16},{16,20},{20,24},{24,28},{28,0},{1,5},{5... | collective-permute-start | bytes 786440 | tf_op jit(solution)/shard_map/while/body/eval_jaxpr/ppermute | solution.py:10
  20.7 10.2 %collective-permute-start = (f32[128,512]{1,0:T(8,128)S(1)}, f32[128,512]{1,0:T(8,128)S(1)}, u32[]{:S(2)}, u32[]{:S(2)}) collective-permute-start(f32[128,512]{1,0:T(8,128)S(1)} %get-tuple-element.190), channel_id=1, source_target_pairs={{0,4},{4,8},{8,12},{12,16},{16,20},{20,24},{24,28},{28,0},{1,5},{5... | collective-permute-start | bytes 786440 | tf_op jit(solution)/shard_map/while/body/eval_jaxpr/ppermute | solution.py:10
  31.7 9.3 %collective-permute-start = (f32[128,512]{1,0:T(8,128)S(1)}, f32[128,512]{1,0:T(8,128)S(1)}, u32[]{:S(2)}, u32[]{:S(2)}) collective-permute-start(f32[128,512]{1,0:T(8,128)S(1)} %get-tuple-element.190), channel_id=1, source_target_pairs={{0,4},{4,8},{8,12},{12,16},{16,20},{20,24},{24,28},{28,0},{1,5},{5... | collective-permute-start | bytes 786440 | tf_op jit(solution)/shard_map/while/body/eval_jaxpr/ppermute | solution.py:10
  41.7 9.1 %collective-permute-start = (f32[128,512]{1,0:T(8,128)S(1)}, f32[128,512]{1,0:T(8,128)S(1)}, u32[]{:S(2)}, u32[]{:S(2)}) collective-permute-start(f32[128,512]{1,0:T(8,128)S(1)} %get-tuple-element.190), channel_id=1, source_target_pairs={{0,4},{4,8},{8,12},{12,16},{16,20},{20,24},{24,28},{28,0},{1,5},{5... | collective-permute-start | bytes 786440 | tf_op jit(solution)/shard_map/while/body/eval_jaxpr/ppermute | solution.py:10
  51.5 9.1 %collective-permute-start = (f32[128,512]{1,0:T(8,128)S(1)}, f32[128,512]{1,0:T(8,128)S(1)}, u32[]{:S(2)}, u32[]{:S(2)}) collective-permute-start(f32[128,512]{1,0:T(8,128)S(1)} %get-tuple-element.190), channel_id=1, source_target_pairs={{0,4},{4,8},{8,12},{12,16},{16,20},{20,24},{24,28},{28,0},{1,5},{5... | collective-permute-start | bytes 786440 | tf_op jit(solution)/shard_map/while/body/eval_jaxpr/ppermute | solution.py:10
  61.3 9.1 %collective-permute-start = (f32[128,512]{1,0:T(8,128)S(1)}, f32[128,512]{1,0:T(8,128)S(1)}, u32[]{:S(2)}, u32[]{:S(2)}) collective-permute-start(f32[128,512]{1,0:T(8,128)S(1)} %get-tuple-element.190), channel_id=1, source_target_pairs={{0,4},{4,8},{8,12},{12,16},{16,20},{20,24},{24,28},{28,0},{1,5},{5... | collective-permute-start | bytes 786440 | tf_op jit(solution)/shard_map/while/body/eval_jaxpr/ppermute | solution.py:10
  71.1 9.1 %collective-permute-start = (f32[128,512]{1,0:T(8,128)S(1)}, f32[128,512]{1,0:T(8,128)S(1)}, u32[]{:S(2)}, u32[]{:S(2)}) collective-permute-start(f32[128,512]{1,0:T(8,128)S(1)} %get-tuple-element.190), channel_id=1, source_target_pairs={{0,4},{4,8},{8,12},{12,16},{16,20},{20,24},{24,28},{28,0},{1,5},{5... | collective-permute-start | bytes 786440 | tf_op jit(solution)/shard_map/while/body/eval_jaxpr/ppermute | solution.py:10
  80.9 37.8 %copy-start = (f32[256,512]{1,0:T(8,128)}, f32[256,512]{1,0:T(8,128)S(1)}, u32[]{:S(2)}) copy-start(f32[256,512]{1,0:T(8,128)S(1)} %get-tuple-element.133) | copy-start | bytes 1572868
where the time goes:
time: 120 us; the launch traced here: 119 us
  waiting for transfers between devices  64.9 us (54%)
  blocking collectives  37.1 us (31%)
  other arithmetic  5.29 us (4%)
  matrix products  5.08 us (4%)
  starting transfers between devices  3.34 us (3%)
  local copies, waits for them, and re-layouts  2.02 us (2%)
    ppermute x7, waiting for transfers between devices, shifted(): return lax.ppermute(value, axis, pairs)  64.9 us
    psum x1, blocking collectives, per_device(): norm_sq = lax.psum(jnp.sum(product * product), ('blk', 'col'))  37.1 us
    dot_general x8, matrix products, times(): jnp.dot(left, right, precision=lax.Precision.HIGHEST, preferred_element_t...  5.08 us
    ppermute x7, starting transfers between devices, shifted(): return lax.ppermute(value, axis, pairs)  3.34 us
  transfers between devices with their start and end apart: 7, of which 7 were waited for; matrix products, arithmetic and copies ran while one was open for 0% of the time, Pallas kernels for 0%

commit v1 on v0

v1 whole, which is shorter than its diff:
```python
import functools

import jax
import jax.numpy as jnp
from jax import lax
from jax.experimental import pallas as pl
from jax.experimental.pallas import tpu as pltpu
from jax.sharding import PartitionSpec as P

MESH = pl.DeviceIdType.MESH
PAIR = 2
CHUNKS = 2
EXTRA = 1


def kernel(
    length,
    cols,
    density,
    hamil,
    occ_p,
    occ_hp,
    window,
    row_window,
    slab,
    groups,
    product,
    norm,
    gathered,
    p_in,
    p_high,
    p_low,
    parts,
    col_parts,
    send_sem,
    recv_sem,
    load_sem,
    part_send,
    part_recv,
    col_send,
    col_recv,
):
    count = length * PAIR
    block, width = hamil.shape
    row_blocks = product.shape[0] // block
    panels = width // block
    piece = block // CHUNKS
    me = lax.axis_index("blk")
    my_col = lax.axis_index("col")
    z = me // PAIR
    x = me % PAIR
    partner = me + 1 - 2 * x
    has_up = z < length - 1
    has_down = z > 0

    load = pltpu.make_async_copy(density, p_in, load_sem)
    load.start()

    barrier = pltpu.get_barrier_semaphore()

    @pl.loop(1, count)
    def greet_blk(step):
        pl.semaphore_signal(
            barrier, inc=1, device_id={"blk": (me + step) % count}, device_id_type=MESH
        )

    @pl.loop(1, cols)
    def greet_col(step):
        pl.semaphore_signal(
            barrier, inc=1, device_id={"col": (my_col + step) % cols}, device_id_type=MESH
        )

    row_at = lax.broadcasted_iota(jnp.int32, (block, block), 0)
    col_at = lax.broadcasted_iota(jnp.int32, (block, block), 1)
    rows_live = row_at < window[me]
    for panel in range(panels):
        size = groups[slab[panel]]
        occupied = occ_hp[0, panel].astype(jnp.float32)
        mask = jnp.where(rows_live & (col_at < size), occupied, 0.0)
        here = pl.ds(panel * block, block)
        gathered[me, :, here] = hamil[:, here] * mask

    pl.semaphore_wait(barrier, count - 1 + cols - 1)

    def move(where, k, chunk, device):
        rows = gathered.at[k, pl.ds(chunk * piece, piece), :]
        return pltpu.make_async_remote_copy(
            src_ref=rows,
            dst_ref=rows,
            send_sem=send_sem.at[where, k, chunk],
            recv_sem=recv_sem.at[k, chunk],
            device_id={"blk": device},
            device_id_type=MESH,
        )

    def up(k, chunk):
        return move(0, k, chunk, me + PAIR)

    def down(k, chunk):
        return move(1, k, chunk, me - PAIR)

    def across(k, chunk):
        return move(2, k, chunk, partner)

    for chunk in range(CHUNKS):
        across(me, chunk).start()

        @pl.when(has_up)
        def _():
            up(me, chunk).start()

        @pl.when(has_down)
        def _():
            down(me, chunk).start()

    load.wait()

    @pl.loop(0, length)
    def split(at):
        for b in range(row_blocks):
            live = row_at < row_window[me * row_blocks + b]
            here = pl.ds(b * block, block)
            for other in range(PAIR):
                k = at * PAIR + other
                mask = jnp.where(
                    live & (col_at < window[k]), occ_p[b, k].astype(jnp.float32), 0.0
                )
                value = p_in[here, pl.ds(pl.multiple_of(k * block, block), block)] * mask
                high = value.astype(jnp.bfloat16)
                there = pl.ds(other * block, block)
                p_high[at, here, there] = high
                p_low[at, here, there] = (value - high.astype(jnp.float32)).astype(jnp.bfloat16)

    def term(at, first):
        right = gathered[pl.ds(at * PAIR, PAIR)].reshape(PAIR * block, width)
        high = right.astype(jnp.bfloat16)
        low = (right - high.astype(jnp.float32)).astype(jnp.bfloat16)

        def times(a, b):
            return jnp.dot(a, b, preferred_element_type=jnp.float32)

        left = p_high[at]
        value = times(left, low) + times(p_low[at], high) + times(left, high)
        product[...] = value if first else product[...] + value

    for chunk in range(CHUNKS):
        across(partner, chunk).wait_recv()
        if chunk < EXTRA:

            @pl.when(has_up)
            def _():
                up(partner, chunk).start()

            @pl.when(has_down)
            def _():
                down(partner, chunk).start()

    term(z, True)

    def pass_on(distance):
        for chunk in range(CHUNKS):

            @pl.when(z - distance >= 0)
            def _():
                k = me - distance * PAIR
                across(k, chunk).wait_recv()

                @pl.when(has_up)
                def _():
                    up(k, chunk).start()

                if chunk < EXTRA:

                    @pl.when(distance > 1)
                    def _():
                        across(k, chunk).start()

                else:
                    across(k, chunk).start()

            @pl.when(z + distance < length)
            def _():
                k = me + distance * PAIR
                across(k, chunk).wait_recv()

                @pl.when(has_down)
                def _():
                    down(k, chunk).start()

                if chunk < EXTRA:

                    @pl.when(distance > 1)
                    def _():
                        across(k, chunk).start()

                else:
                    across(k, chunk).start()

    def add_terms(distance):
        for sign in (-1, 1):
            at = z + sign * distance

            @pl.when((at >= 0) & (at < length))
            def _():
                for chunk in range(CHUNKS):
                    across(partner + sign * distance * PAIR, chunk).wait_recv()
                term(at, False)

    if length > 1:
        pass_on(1)

    @pl.loop(2, length)
    def steps(distance):
        pass_on(distance)
        add_terms(distance - 1)

    if length > 1:
        add_terms(length - 1)

    squares = product[...] * product[...]
    squares = jnp.sum(squares.reshape(squares.shape[0] // 8, 8, width), axis=0)
    total = squares[:, :128]
    for panel in range(1, width // 128):
        total = total + squares[:, panel * 128 : (panel + 1) * 128]
    parts[me] = total

    def part_to(device):
        return pltpu.make_async_remote_copy(
            src_ref=parts.at[me],
            dst_ref=parts.at[me],
            send_sem=part_send.at[device],
            recv_sem=part_recv.at[me],
            device_id={"blk": device},
            device_id_type=MESH,
        )

    def part_from(device):
        return pltpu.make_async_remote_copy(
            src_ref=parts.at[device],
            dst_ref=parts.at[device],
            send_sem=part_send.at[device],
            recv_sem=part_recv.at[device],
            device_id={"blk": device},
            device_id_type=MESH,
        )

    @pl.loop(1, count)
    def send_parts(step):
        part_to((me + step) % count).start()

    @pl.loop(0, length)
    def sent(at):
        k = at * PAIR + x
        far = (at - z > 1) | (z - at > 1) | (at == z)
        for chunk in range(CHUNKS):

            @pl.when(has_up & (at <= z))
            def _():
                up(k, chunk).wait_send()

            @pl.when(has_down & (at >= z))
            def _():
                down(k, chunk).wait_send()

            if chunk < EXTRA:

                @pl.when(far)
                def _():
                    across(k, chunk).wait_send()

            else:
                across(k, chunk).wait_send()

    for chunk in range(EXTRA):

        @pl.when(has_up)
        def _():
            up(partner, chunk).wait_send()

        @pl.when(has_down)
        def _():
            down(partner, chunk).wait_send()

    @pl.loop(1, count)
    def get_parts(step):
        part_from((me + step) % count).wait_recv()

    col_parts[my_col] = jnp.sum(parts[...], axis=0)

    def col_to(device):
        return pltpu.make_async_remote_copy(
            src_ref=col_parts.at[my_col],
            dst_ref=col_parts.at[my_col],
            send_sem=col_send.at[device],
            recv_sem=col_recv.at[my_col],
            device_id={"col": device},
            device_id_type=MESH,
        )

    def col_from(device):
        return pltpu.make_async_remote_copy(
            src_ref=col_parts.at[device],
            dst_ref=col_parts.at[device],
            send_sem=col_send.at[device],
            recv_sem=col_recv.at[device],
            device_id={"col": device},
            device_id_type=MESH,
        )

    @pl.loop(1, cols)
    def send_cols(step):
        col_to((my_col + step) % cols).start()

    @pl.loop(1, count)
    def sent_parts(step):
        part_to((me + step) % count).wait_send()

    @pl.loop(1, cols)
    def get_cols(step):
        col_from((my_col + step) % cols).wait_recv()

    norm[0] = jnp.sum(jnp.sum(col_parts[...], axis=0))

    @pl.loop(1, cols)
    def sent_cols(step):
        col_to((my_col + step) % cols).wait_send()


def solution(mesh):
    count = mesh.shape["blk"]
    cols = mesh.shape["col"]
    length = count // PAIR

    def per_device(
        density,
        occupied_p,
        hamil_dens,
        occupied_hp,
        window_sizes,
        row_window_sizes,
        slab_index,
        group_sizes,
    ):
        rows, inner = density.shape
        block, width = hamil_dens.shape
        vmem = pl.BlockSpec(memory_space=pltpu.VMEM)
        smem = pl.BlockSpec(memory_space=pltpu.SMEM)
        product, norm = pl.pallas_call(
            functools.partial(kernel, length, cols),
            out_shape=(
                jax.ShapeDtypeStruct((rows, width), jnp.float32),
                jax.ShapeDtypeStruct((1,), jnp.float32),
            ),
            in_specs=[pl.BlockSpec(memory_space=pltpu.HBM), vmem] + [smem] * 6,
            out_specs=(vmem, smem),
            scratch_shapes=[
                pltpu.VMEM((count, block, width), jnp.float32),
                pltpu.VMEM((rows, inner), jnp.float32),
                pltpu.VMEM((length, rows, PAIR * block), jnp.bfloat16),
                pltpu.VMEM((length, rows, PAIR * block), jnp.bfloat16),
                pltpu.VMEM((count, 8, 128), jnp.float32),
                pltpu.VMEM((cols, 8, 128), jnp.float32),
                pltpu.SemaphoreType.DMA((3, count, CHUNKS)),
                pltpu.SemaphoreType.DMA((count, CHUNKS)),
                pltpu.SemaphoreType.DMA,
                pltpu.SemaphoreType.DMA((count,)),
                pltpu.SemaphoreType.DMA((count,)),
                pltpu.SemaphoreType.DMA((cols,)),
                pltpu.SemaphoreType.DMA((cols,)),
            ],
            compiler_params=pltpu.CompilerParams(
                collective_id=0, has_side_effects=True, vmem_limit_bytes=48 << 20
            ),
        )(
            density,
            hamil_dens,
            occupied_p,
            occupied_hp,
            window_sizes,
            row_window_sizes,
            slab_index,
            group_sizes,
        )
        return product, norm.reshape(())

    return jax.shard_map(
        per_device,
        mesh=mesh,
        in_specs=(
            P("blk", None),
            P("blk", None),
            P("blk", "col"),
            P("blk", "col"),
            P(),
            P(),
            P("col"),
            P(),
        ),
        out_specs=(P("blk", "col"), P()),
        check_vma=False,
    )
```

time: 120 us -> 50.9 us (0.42)
  waiting for transfers between devices: 64.9 us -> 0 us
  Pallas kernels: 0 us -> 41.1 us
  blocking collectives: 37.1 us -> 0 us
  other arithmetic: 5.29 us -> 0 us
  matrix products: 5.08 us -> 0 us
  local copies, waits for them, and re-layouts: 2.02 us -> 6.95 us
  starting transfers between devices: 3.34 us -> 0 us
  between operations: 0.7 us -> 2.47 us
    ppermute x7 -> x0, waiting for transfers between devices: 64.9 us -> none  [shifted(): return lax.ppermute(value, axis, pairs)]
    pallas_call x0 -> x1, Pallas kernels: none -> 41.1 us  [per_device(): pl.pallas_call(functools.partial(kernel, length, cols), out_shape=(jax.Sh...]
    psum x1 -> x0, blocking collectives: 37.1 us -> none  [per_device(): norm_sq = lax.psum(jnp.sum(product * product), ('blk', 'col'))]
    unnamed x4 -> x17, local copies, waits for them, and re-layouts: 0.01 us -> 6.95 us
    dot_general x8 -> x0, matrix products: 5.08 us -> none  [times(): jnp.dot(left, right, precision=lax.Precision.HIGHEST, preferred_element_t...]
    ppermute x7 -> x0, starting transfers between devices: 3.34 us -> none  [shifted(): return lax.ppermute(value, axis, pairs)]
    convert_element_type x5 -> x0, other arithmetic: 2.14 us -> none  [the longest x2 0.73 us: per_device(): inner_live = (offsets[None, :] < window_sizes[:, None]).astype(jnp.float32)]
    reduce_sum x2 -> x0, other arithmetic: 1.61 us -> none  [the longest x1 0.87 us: per_device(): jnp.sum(jnp.where(slab_index[:, None] == groups[None, :], group_sizes[Non...]
  transfers between devices with their start and end apart: 7 -> 0, of which waited for: 7 -> 0; matrix products, arithmetic and copies ran while one was open for 0% -> 0% of each run, Pallas kernels for 0% -> 0%
where the time goes in v1:
time: 50.9 us; the launch traced here: 50.6 us
  Pallas kernels  41.1 us (81%)
  local copies, waits for them, and re-layouts  6.95 us (14%)
  between operations  2.47 us (5%)
    pallas_call x1, Pallas kernels, per_device(): pl.pallas_call(functools.partial(kernel, length, cols), out_shape=(jax.Sh...  41.1 us
    unnamed x17, local copies, waits for them, and re-layouts  6.95 us

profile of v1, /device:TPU:0, one launch (start us, length us, event | category | flops | bytes accessed | tf_op | source)
XLA Modules:
  0.0 50.6 jit_solution(10187418650786835721)
XLA Ops:
  0.6 0.0 copy-start
  0.6 1.2 %copy-done = f32[256,1024]{1,0:T(8,128)S(1)} copy-done((f32[256,1024]{1,0:T(8,128)S(1)}, f32[256,1024]{1,0:T(8,128)}, u32[]{:S(2)}) %copy-start) | copy-done | bytes 1048600
  1.9 0.0 copy-start.1
  1.9 0.9 %copy-done.1 = f32[128,512]{1,0:T(8,128)S(1)} copy-done((f32[128,512]{1,0:T(8,128)S(1)}, f32[128,512]{1,0:T(8,128)}, u32[]{:S(2)}) %copy-start.1) | copy-done | bytes 262168
  2.8 0.0 copy-start.2
  2.8 0.7 %copy-done.2 = s32[782]{0:T(1024)S(1)} copy-done((s32[782]{0:T(1024)S(1)}, s32[782]{0:T(1024)}, u32[]{:S(2)}) %copy-start.2) | copy-done | bytes 3152
  3.5 0.0 copy-start.3
  3.5 0.7 %copy-done.3 = s32[2,8]{1,0:T(2,128)S(1)} copy-done((s32[2,8]{1,0:T(2,128)S(1)}, s32[2,8]{1,0:T(2,128)}, u32[]{:S(2)}) %copy-start.3) | copy-done | bytes 88
  4.2 0.0 copy-start.4
  4.2 0.7 %copy-done.4 = s32[1,4]{1,0:T(1,128)S(1)} copy-done((s32[1,4]{1,0:T(1,128)S(1)}, s32[1,4]{1,0:T(1,128)}, u32[]{:S(2)}) %copy-start.4) | copy-done | bytes 40
  4.8 0.0 copy-start.5
  4.8 0.7 %copy-done.5 = s32[8]{0:T(128)S(1)} copy-done((s32[8]{0:T(128)S(1)}, s32[8]{0:T(128)}, u32[]{:S(2)}) %copy-start.5) | copy-done | bytes 56
  5.5 0.0 copy-start.6
  5.5 0.7 %copy-done.6 = s32[16]{0:T(128)S(1)} copy-done((s32[16]{0:T(128)S(1)}, s32[16]{0:T(128)}, u32[]{:S(2)}) %copy-start.6) | copy-done | bytes 88
  6.1 0.0 copy-start.7
  6.1 0.7 %copy-done.7 = s32[4]{0:T(128)S(1)} copy-done((s32[4]{0:T(128)S(1)}, s32[4]{0:T(128)}, u32[]{:S(2)}) %copy-start.7) | copy-done | bytes 40
  6.8 41.1 %shard_map.95 = (f32[256,512]{1,0:T(8,128)S(1)}, f32[1]{0:T(128)}) custom-call(f32[256,1024]{1,0:T(8,128)S(1)} %copy-done, f32[128,512]{1,0:T(8,128)S(1)} %copy-done.1, s32[2,8]{1,0:T(2,128)S(1)} %copy-done.3, s32[1,4]{1,0:T(1,128)S(1)} %copy-done.4, s32[8]{0:T(128)S(1)} %copy-done.5, s32[16]{0:T(128)S(1)} %copy-done.6, s32[4]{0:T(128)S(1)} %copy-done.7, ...), custom_call_target="tpu_custom_call" | custom-call | tf_op jit(solution)/shard_map/pallas_call | solution.py:348
  48.0 0.8 %copy.12 = f32[256,512]{1,0:T(8,128)} copy(f32[256,512]{1,0:T(8,128)S(1)} %get-tuple-element.8) | data formatting | bytes 1048576
Async XLA Ops:
  0.6 1.2 %copy-start = (f32[256,1024]{1,0:T(8,128)S(1)}, f32[256,1024]{1,0:T(8,128)}, u32[]{:S(2)}) copy-start(f32[256,1024]{1,0:T(8,128)} %density.1) | copy-start | bytes 3145732
  1.9 0.9 %copy-start.1 = (f32[128,512]{1,0:T(8,128)S(1)}, f32[128,512]{1,0:T(8,128)}, u32[]{:S(2)}) copy-start(f32[128,512]{1,0:T(8,128)} %hamil.1) | copy-start | bytes 786436
  2.8 0.7 %copy-start.2 = (s32[782]{0:T(1024)S(1)}, s32[782]{0:T(1024)}, u32[]{:S(2)}) copy-start(s32[782]{0:T(1024)} %groups.1) | copy-start | bytes 9388
  3.5 0.7 %copy-start.3 = (s32[2,8]{1,0:T(2,128)S(1)}, s32[2,8]{1,0:T(2,128)}, u32[]{:S(2)}) copy-start(s32[2,8]{1,0:T(2,128)} %occ_p.1) | copy-start | bytes 196
  4.2 0.7 %copy-start.4 = (s32[1,4]{1,0:T(1,128)S(1)}, s32[1,4]{1,0:T(1,128)}, u32[]{:S(2)}) copy-start(s32[1,4]{1,0:T(1,128)} %occ_hp.1) | copy-start | bytes 52
  4.8 0.7 %copy-start.5 = (s32[8]{0:T(128)S(1)}, s32[8]{0:T(128)}, u32[]{:S(2)}) copy-start(s32[8]{0:T(128)} %window.1) | copy-start | bytes 100
  5.5 0.7 %copy-start.6 = (s32[16]{0:T(128)S(1)}, s32[16]{0:T(128)}, u32[]{:S(2)}) copy-start(s32[16]{0:T(128)} %row_window.1) | copy-start | bytes 196
  6.1 0.7 %copy-start.7 = (s32[4]{0:T(128)S(1)}, s32[4]{0:T(128)}, u32[]{:S(2)}) copy-start(s32[4]{0:T(128)} %slab.1) | copy-start | bytes 52

commit v2 on v1

--- a/solution.py
+++ b/solution.py
@@ -9,7 +9,7 @@
 
 MESH = pl.DeviceIdType.MESH
 PAIR = 2
-CHUNKS = 2
+CHUNKS = 4
 EXTRA = 1
 
 
@@ -17,6 +17,16 @@
     length,
     cols,
     density,
+    hamil_in,
+    occ_p_in,
+    occ_hp_in,
+    window_in,
+    row_window_in,
+    slab_in,
+    groups_in,
+    product_out,
+    norm,
+    product,
     hamil,
     occ_p,
     occ_hp,
@@ -24,8 +34,6 @@
     row_window,
     slab,
     groups,
-    product,
-    norm,
     gathered,
     p_in,
     p_high,
@@ -53,9 +61,21 @@
     has_up = z < length - 1
     has_down = z > 0
 
-    load = pltpu.make_async_copy(density, p_in, load_sem)
-    load.start()
-
+    loads = [
+        pltpu.make_async_copy(source, target, load_sem.at[at])
+        for at, (source, target) in enumerate(
+            (
+                (hamil_in, hamil),
+                (occ_hp_in, occ_hp),
+                (window_in, window),
+                (slab_in, slab),
+                (groups_in, groups),
+                (row_window_in, row_window),
+                (occ_p_in, occ_p),
+                (density, p_in),
+            )
+        )
+    ]
     barrier = pltpu.get_barrier_semaphore()
 
     @pl.loop(1, count)
@@ -69,6 +89,12 @@
         pl.semaphore_signal(
             barrier, inc=1, device_id={"col": (my_col + step) % cols}, device_id_type=MESH
         )
+
+    for load in loads:
+        load.start()
+
+    for load in loads[:5]:
+        load.wait()
 
     row_at = lax.broadcasted_iota(jnp.int32, (block, block), 0)
     col_at = lax.broadcasted_iota(jnp.int32, (block, block), 1)
@@ -113,7 +139,8 @@
         def _():
             down(me, chunk).start()
 
-    load.wait()
+    for load in loads[5:]:
+        load.wait()
 
     @pl.loop(0, length)
     def split(at):
@@ -217,6 +244,9 @@
     if length > 1:
         add_terms(length - 1)
 
+    store = pltpu.make_async_copy(product, product_out, load_sem.at[0])
+    store.start()
+
     squares = product[...] * product[...]
     squares = jnp.sum(squares.reshape(squares.shape[0] // 8, 8, width), axis=0)
     total = squares[:, :128]
@@ -319,6 +349,7 @@
     def get_cols(step):
         col_from((my_col + step) % cols).wait_recv()
 
+    store.wait()
     norm[0] = jnp.sum(jnp.sum(col_parts[...], axis=0))
 
     @pl.loop(1, cols)
@@ -343,7 +374,7 @@
     ):
         rows, inner = density.shape
         block, width = hamil_dens.shape
-        vmem = pl.BlockSpec(memory_space=pltpu.VMEM)
+        hbm = pl.BlockSpec(memory_space=pltpu.HBM)
         smem = pl.BlockSpec(memory_space=pltpu.SMEM)
         product, norm = pl.pallas_call(
             functools.partial(kernel, length, cols),
@@ -351,9 +382,17 @@
                 jax.ShapeDtypeStruct((rows, width), jnp.float32),
                 jax.ShapeDtypeStruct((1,), jnp.float32),
             ),
-            in_specs=[pl.BlockSpec(memory_space=pltpu.HBM), vmem] + [smem] * 6,
-            out_specs=(vmem, smem),
+            in_specs=[hbm] * 8,
+            out_specs=(hbm, smem),
             scratch_shapes=[
+                pltpu.VMEM((rows, width), jnp.float32),
+                pltpu.VMEM((block, width), jnp.float32),
+                pltpu.SMEM(occupied_p.shape, jnp.int32),
+                pltpu.SMEM(occupied_hp.shape, jnp.int32),
+                pltpu.SMEM(window_sizes.shape, jnp.int32),
+                pltpu.SMEM(row_window_sizes.shape, jnp.int32),
+                pltpu.SMEM(slab_index.shape, jnp.int32),
+                pltpu.SMEM(group_sizes.shape, jnp.int32),
                 pltpu.VMEM((count, block, width), jnp.float32),
                 pltpu.VMEM((rows, inner), jnp.float32),
                 pltpu.VMEM((length, rows, PAIR * block), jnp.bfloat16),
@@ -362,14 +401,14 @@
                 pltpu.VMEM((cols, 8, 128), jnp.float32),
                 pltpu.SemaphoreType.DMA((3, count, CHUNKS)),
                 pltpu.SemaphoreType.DMA((count, CHUNKS)),
-                pltpu.SemaphoreType.DMA,
+                pltpu.SemaphoreType.DMA((8,)),
                 pltpu.SemaphoreType.DMA((count,)),
                 pltpu.SemaphoreType.DMA((count,)),
                 pltpu.SemaphoreType.DMA((cols,)),
                 pltpu.SemaphoreType.DMA((cols,)),
             ],
             compiler_params=pltpu.CompilerParams(
-                collective_id=0, has_side_effects=True, vmem_limit_bytes=48 << 20
+                collective_id=0, has_side_effects=True, vmem_limit_bytes=56 << 20
             ),
         )(
             density,

time: 50.9 us -> 43.3 us (0.85)
  local copies, waits for them, and re-layouts: 6.95 us -> 1.87 us
  Pallas kernels: 41.1 us -> 38.8 us
    unnamed x17 -> x1, local copies, waits for them, and re-layouts: 6.95 us -> 1.87 us
    pallas_call x1, Pallas kernels: 41.1 us -> 38.8 us  [per_device(): pl.pallas_call(functools.partial(kernel, length, cols), out_shape=(jax.Sh...]
where the time goes in v2:
time: 43.3 us; the launch traced here: 43.1 us
  Pallas kernels  38.8 us (90%)
  between operations  2.34 us (5%)
  local copies, waits for them, and re-layouts  1.87 us (4%)
    pallas_call x1, Pallas kernels, per_device(): pl.pallas_call(functools.partial(kernel, length, cols), out_shape=(jax.Sh...  38.8 us
    unnamed x1, local copies, waits for them, and re-layouts  1.87 us

profile of v2, /device:TPU:0, one launch (start us, length us, event | category | flops | bytes accessed | tf_op | source)
XLA Modules:
  0.0 43.1 jit_solution(17123553084586955159)
XLA Ops:
  0.6 38.8 %shard_map.95 = (f32[256,512]{1,0:T(8,128)}, f32[1]{0:T(128)}) custom-call(f32[256,1024]{1,0:T(8,128)} %density.1, f32[128,512]{1,0:T(8,128)} %hamil_in.1, s32[2,8]{1,0:T(2,128)} %occ_p_in.1, s32[1,4]{1,0:T(1,128)} %occ_hp_in.1, s32[8]{0:T(128)} %window_in.1, s32[16]{0:T(128)} %row_window_in.1, s32[4]{0:T(128)} %slab_in.1, s32[782]{0:T(1024)} %groups_in.1), custom_call_target="tpu_custom_call" | custom-call | tf_op jit(solution)/shard_map/pallas_call | solution.py:379
  39.5 1.9 %copy.12 = f32[256,512]{1,0:T(8,128)} copy(f32[256,512]{1,0:T(8,128)} %get-tuple-element.8) | data formatting | bytes 1048576

commit v3 on v2

--- a/solution.py
+++ b/solution.py
@@ -170,19 +170,16 @@
         value = times(left, low) + times(p_low[at], high) + times(left, high)
         product[...] = value if first else product[...] + value
 
-    for chunk in range(CHUNKS):
+    for chunk in range(EXTRA):
         across(partner, chunk).wait_recv()
-        if chunk < EXTRA:
-
-            @pl.when(has_up)
-            def _():
-                up(partner, chunk).start()
-
-            @pl.when(has_down)
-            def _():
-                down(partner, chunk).start()
-
-    term(z, True)
+
+        @pl.when(has_up)
+        def _():
+            up(partner, chunk).start()
+
+        @pl.when(has_down)
+        def _():
+            down(partner, chunk).start()
 
     def pass_on(distance):
         for chunk in range(CHUNKS):
@@ -236,13 +233,17 @@
     if length > 1:
         pass_on(1)
 
+    for chunk in range(EXTRA, CHUNKS):
+        across(partner, chunk).wait_recv()
+    term(z, True)
+
     @pl.loop(2, length)
     def steps(distance):
         pass_on(distance)
-        add_terms(distance - 1)
-
-    if length > 1:
-        add_terms(length - 1)
+
+    @pl.loop(1, length)
+    def products(distance):
+        add_terms(distance)
 
     store = pltpu.make_async_copy(product, product_out, load_sem.at[0])
     store.start()

time: 43.3 us -> 42.6 us (0.984)
  Pallas kernels: 38.8 us -> 38.2 us
    pallas_call x1, Pallas kernels: 38.8 us -> 38.2 us  [per_device(): pl.pallas_call(functools.partial(kernel, length, cols), out_shape=(jax.Sh...]
where the time goes in v3:
time: 42.6 us; the launch traced here: 42.4 us
  Pallas kernels  38.2 us (90%)
  between operations  2.34 us (5%)
  local copies, waits for them, and re-layouts  1.87 us (4%)
    pallas_call x1, Pallas kernels, per_device(): pl.pallas_call(functools.partial(kernel, length, cols), out_shape=(jax.Sh...  38.2 us
    unnamed x1, local copies, waits for them, and re-layouts  1.87 us

profile of v3, /device:TPU:0, one launch (start us, length us, event | category | flops | bytes accessed | tf_op | source)
XLA Modules:
  0.0 42.4 jit_solution(3578357559068543912)
XLA Ops:
  0.6 38.2 %shard_map.95 = (f32[256,512]{1,0:T(8,128)}, f32[1]{0:T(128)}) custom-call(f32[256,1024]{1,0:T(8,128)} %density.1, f32[128,512]{1,0:T(8,128)} %hamil_in.1, s32[2,8]{1,0:T(2,128)} %occ_p_in.1, s32[1,4]{1,0:T(1,128)} %occ_hp_in.1, s32[8]{0:T(128)} %window_in.1, s32[16]{0:T(128)} %row_window_in.1, s32[4]{0:T(128)} %slab_in.1, s32[782]{0:T(1024)} %groups_in.1), custom_call_target="tpu_custom_call" | custom-call | tf_op jit(solution)/shard_map/pallas_call | solution.py:380
  38.8 1.9 %copy.12 = f32[256,512]{1,0:T(8,128)} copy(f32[256,512]{1,0:T(8,128)} %get-tuple-element.8) | data formatting | bytes 1048576
